TPU v7x, 32 devices: a whole 2x2x4 slice. The times are simulated.
32 devices in a mesh: body: 2 (over y), row: 4 (over x, core), col: 4 (over z).
Axes of the slice: x: 2, y: 2, z: 4, core: 2. Of those that a mesh axis runs over, the one named last changes fastest.
Arguments:
- lam_start: float32 [2, 128, 16384], P('body', None, ('row', 'col')), may hold values from -8 to 8
- load: float32 [2, 128, 16384], P('body', None, ('row', 'col')), may hold values from -24 to 24
- operator: bfloat16 [2, 16384, 4, 4, 1024], P('body', 'row', None, 'col'), as said below
- partner: int32 [2, 16384], P('body', ('row', 'col')), may hold values from 0 to 16383, as said below
- active: int32 [16384], P(('row', 'col')), may hold values 0 or 1
- bounds: int32 [2, 2], P('body'), may hold values from 1 to 20, as said below
Outputs:
- multipliers: float32 [2, 128, 16384], P('body', None, ('row', 'col'))
- residual: float32 [2, 128, 16384], P('body', None, ('row', 'col'))
Inputs may be any that keep to these rules, and one draw needn't show every extreme that they name: Each operator F_b is symmetric, with positive diagonal. partner[0] maps every aligned block of 1024 unknowns onto itself, one to one, and partner[1] is its inverse: partner[1, partner[0, i]] = i. bounds[b, 0] is 1 or 2 and bounds[b, 1] is 18 to 20.
All inputs are finite; a program needn't handle non-finite values. No bound on the sum of `active` on one device may be relied on, other than what follows from the above.
Results may differ from a plain program's by a relative error of at most 0.03.
The roundings to bfloat16 on the way count: a program that leaves them out, or rounds other values in their place, can miss the bound.
Values may be sent and summed in bfloat16 or wider, within the bound.
A program may use at most 128 MiB of HBM per device.

v0:
```python
import jax
import jax.numpy as jnp
from jax import lax
from jax.sharding import PartitionSpec as P

K = 4


def swapped(value, axis, distance):
    mask = 2**distance
    pairs = [(source, source ^ mask) for source in range(lax.axis_size(axis))]
    return lax.ppermute(value, axis, pairs)


def clamp_local(lam, partner, active):
    peer = swapped(lam, "body", 0)
    width = lam.shape[1]
    local = partner % width
    mate = jnp.take(peer, local, axis=1)
    which = lax.axis_index("body")
    sign = (1 - 2 * which).astype(jnp.float32)
    flag_index = jnp.where(which == 0, jnp.arange(width, dtype=jnp.int32), local)
    flags = jnp.take(active, flag_index) > 0
    middle = 0.5 * (lam + mate)
    normal = 0.5 * sign * (lam - mate)
    normal = jnp.where(flags[None, :], jnp.maximum(normal, 0.0), normal)
    return middle + sign * normal


def apply_tile(field, tile):
    rounded = field.astype(jnp.bfloat16)
    partial_sum = jnp.dot(
        lax.all_gather(rounded, "col", axis=1, tiled=True), tile, preferred_element_type=jnp.float32
    )
    return lax.psum_scatter(partial_sum, "row", scatter_dimension=1, tiled=True)


def cheb_local(start, load, tile, lower, upper):
    theta = 0.5 * (upper + lower)
    delta = 0.5 * (upper - lower)
    sigma = theta / delta
    answer = start
    resid = load - apply_tile(answer, tile)
    direction = resid / theta
    rho = delta / theta
    for step in range(K):
        answer = answer + direction
        resid = resid - apply_tile(direction, tile)
        if step + 1 < K:
            rho_new = 1.0 / (2.0 * sigma - rho)
            direction = rho_new * rho * direction + 2.0 * rho_new / delta * resid
            rho = rho_new
    return (answer, resid)


def per_device(lam_start, load, operator, partner, active, bounds):
    tile = operator.reshape(operator.shape[1], operator.shape[2] * operator.shape[4])
    lower = bounds[0, 0].astype(jnp.float32)
    upper = bounds[0, 1].astype(jnp.float32)
    own_load = load[0]
    own_partner = partner[0]
    first = clamp_local(lam_start[0], own_partner, active)
    second, unused = cheb_local(first, own_load, tile, lower, upper)
    third = clamp_local(second, own_partner, active)
    answer, resid = cheb_local(third, own_load, tile, lower, upper)
    return (answer[None], resid[None])


def solution(mesh):
    return jax.shard_map(
        per_device,
        mesh=mesh,
        in_specs=(
            P("body", None, ("row", "col")),
            P("body", None, ("row", "col")),
            P("body", "row", None, "col", None),
            P("body", ("row", "col")),
            P(("row", "col")),
            P("body", None),
        ),
        out_specs=(P("body", None, ("row", "col")), P("body", None, ("row", "col"))),
        check_vma=False,
    )
```

profile of v0, /device:TPU:0, one launch (start us, length us, event | category | flops | bytes accessed | tf_op | source)
XLA Modules:
  0.0 756.1 jit_solution(8804111611646040820)
XLA Ops:
  7.2 3.0 collective-permute-start
  10.3 0.7 fusion.15
  11.0 4.5 gather_fusion.1
  15.5 0.7 compare_and_fusion
  16.2 6.2 collective-permute-done
  22.4 0.2 copy.12
  22.6 2.8 gather_fusion
  25.4 0.2 copy.13
  25.6 1.9 fusion.18
  27.6 22.7 %copy.16 = bf16[512,8,4,1024]{3,1,2,0:T(8,128)(2,1)} copy(bf16[512,8,4,1024]{3,2,1,0:T(4,128)(2,1)} %bitcast.89) | data formatting | bytes 67108864
  50.4 6.8 all-gather.10.cloned.1.call-done
  57.1 16.7 %fusion.25 = f32[128,4096]{1,0:T(8,128)} fusion(bf16[128,4096]{1,0:T(8,128)(2,1)} %all-gather.10.cloned.1.call-done, bf16[4096,4096]{1,0:T(8,128)(2,1)} %bitcast.80), kind=kOutput, calls=%fused_computation.51 | convolution fusion | flops 4294967296 | bytes 36700160 | tf_op jit(solution)/shard_map/dot_general | solution.py:32
  73.9 0.0 all-gather.12.cloned.1.call-start
  73.9 0.6 fusion.24
  75.8 29.1 %reduce-scatter.10.cloned.1.call-done = f32[128,1024]{1,0:T(8,128)} async-done(((f32[128,4096]{1,0:T(8,128)}), f32[128,1024]{1,0:T(8,128)}) %reduce-scatter.10.cloned.1.call-update) | async-done | bytes 524304 | tf_op jit(solution)/shard_map/reduce_scatter | solution.py:35
  105.0 1.9 fusion.23
  106.9 0.5 reduce-scatter.12.cloned.1.call-start
  107.4 27.7 %all-gather.12.cloned.1.call-done = bf16[128,4096]{1,0:T(8,128)(2,1)} async-done(((bf16[128,1024]{1,0:T(8,128)(2,1)}), bf16[128,4096]{1,0:T(8,128)(2,1)}) %all-gather.12.cloned.1.call-update) | async-done | bytes 1048592 | tf_op jit(solution)/shard_map/all_gather | solution.py:33
  135.2 16.7 %fusion.26 = f32[128,4096]{1,0:T(8,128)} fusion(bf16[128,4096]{1,0:T(8,128)(2,1)} %all-gather.12.cloned.1.call-done, bf16[4096,4096]{1,0:T(8,128)(2,1)} %bitcast.81), kind=kOutput, calls=%fused_computation.52 | convolution fusion | flops 4294967296 | bytes 36700160 | tf_op jit(solution)/shard_map/dot_general | solution.py:32
  151.9 0.0 all-gather.14.cloned.1.call-start
  152.1 30.8 %reduce-scatter.12.cloned.1.call-done = f32[128,1024]{1,0:T(8,128)} async-done(((f32[128,4096]{1,0:T(8,128)}), f32[128,1024]{1,0:T(8,128)}) %reduce-scatter.12.cloned.1.call-update) | async-done | bytes 524304 | tf_op jit(solution)/shard_map/reduce_scatter | solution.py:35
  183.0 2.0 fusion.12
  184.9 0.0 reduce-scatter.14.cloned.1.call-start
  185.0 28.0 %all-gather.14.cloned.1.call-done = bf16[128,4096]{1,0:T(8,128)(2,1)} async-done(((bf16[128,1024]{1,0:T(8,128)(2,1)}), bf16[128,4096]{1,0:T(8,128)(2,1)}) %all-gather.14.cloned.1.call-update) | async-done | bytes 1048592 | tf_op jit(solution)/shard_map/all_gather | solution.py:33
  213.0 16.7 %fusion.27 = f32[128,4096]{1,0:T(8,128)} fusion(bf16[128,4096]{1,0:T(8,128)(2,1)} %all-gather.14.cloned.1.call-done, bf16[4096,4096]{1,0:T(8,128)(2,1)} %bitcast.82), kind=kOutput, calls=%fused_computation.53 | convolution fusion | flops 4294967296 | bytes 36700160 | tf_op jit(solution)/shard_map/dot_general | solution.py:32
  229.8 0.0 all-gather.16.cloned.1.call-start
  229.9 30.9 %reduce-scatter.14.cloned.1.call-done = f32[128,1024]{1,0:T(8,128)} async-done(((f32[128,4096]{1,0:T(8,128)}), f32[128,1024]{1,0:T(8,128)}) %reduce-scatter.14.cloned.1.call-update) | async-done | bytes 524304 | tf_op jit(solution)/shard_map/reduce_scatter | solution.py:35
  260.9 2.1 fusion.8
  263.0 0.2 reduce-scatter.16.cloned.1.call-start
  263.2 27.9 %all-gather.16.cloned.1.call-done = bf16[128,4096]{1,0:T(8,128)(2,1)} async-done(((bf16[128,1024]{1,0:T(8,128)(2,1)}), bf16[128,4096]{1,0:T(8,128)(2,1)}) %all-gather.16.cloned.1.call-update) | async-done | bytes 1048592 | tf_op jit(solution)/shard_map/all_gather | solution.py:33
  291.1 16.7 %fusion.28 = f32[128,4096]{1,0:T(8,128)} fusion(bf16[128,4096]{1,0:T(8,128)(2,1)} %all-gather.16.cloned.1.call-done, bf16[4096,4096]{1,0:T(8,128)(2,1)} %bitcast.83), kind=kOutput, calls=%fused_computation.54 | convolution fusion | flops 4294967296 | bytes 36700160 | tf_op jit(solution)/shard_map/dot_general | solution.py:32
  307.8 0.0 all-gather.18.cloned.1.call-start
  308.0 30.9 %reduce-scatter.16.cloned.1.call-done = f32[128,1024]{1,0:T(8,128)} async-done(((f32[128,4096]{1,0:T(8,128)}), f32[128,1024]{1,0:T(8,128)}) %reduce-scatter.16.cloned.1.call-update) | async-done | bytes 524304 | tf_op jit(solution)/shard_map/reduce_scatter | solution.py:35
  338.9 1.7 add_add_fusion
  340.6 1.5 collective-permute-start.1
  342.1 12.2 %collective-permute-done.1 = f32[128,1024]{1,0:T(8,128)S(1)} collective-permute-done((f32[128,1024]{1,0:T(8,128)S(1)}, f32[128,1024]{1,0:T(8,128)S(1)}, u32[]{:S(2)}, u32[]{:S(2)}) %collective-permute-start.1) | collective-permute-done | bytes 524320 | tf_op jit(solution)/shard_map/ppermute | solution.py:12
  354.3 0.2 copy.14
  354.5 2.8 gather_fusion.2
  357.4 0.2 copy.15
  357.6 0.9 fusion.17
  358.5 0.0 reduce-scatter.18.cloned.1.call-start
  358.5 28.0 %all-gather.18.cloned.1.call-done = bf16[128,4096]{1,0:T(8,128)(2,1)} async-done(((bf16[128,1024]{1,0:T(8,128)(2,1)}), bf16[128,4096]{1,0:T(8,128)(2,1)}) %all-gather.18.cloned.1.call-update) | async-done | bytes 1048592 | tf_op jit(solution)/shard_map/all_gather | solution.py:33
  386.6 16.7 %fusion.29 = f32[128,4096]{1,0:T(8,128)} fusion(bf16[128,4096]{1,0:T(8,128)(2,1)} %all-gather.18.cloned.1.call-done, bf16[4096,4096]{1,0:T(8,128)(2,1)} %bitcast.84), kind=kOutput, calls=%fused_computation.55 | convolution fusion | flops 4294967296 | bytes 36700160 | tf_op jit(solution)/shard_map/dot_general | solution.py:32
  403.3 0.0 all-gather.20.cloned.1.call-start
  403.3 31.0 %reduce-scatter.18.cloned.1.call-done = f32[128,1024]{1,0:T(8,128)} async-done(((f32[128,4096]{1,0:T(8,128)}), f32[128,1024]{1,0:T(8,128)}) %reduce-scatter.18.cloned.1.call-update) | async-done | bytes 524304 | tf_op jit(solution)/shard_map/reduce_scatter | solution.py:35
  434.4 1.9 fusion.21
  436.3 0.3 reduce-scatter.20.cloned.1.call-start
  436.6 28.0 %all-gather.20.cloned.1.call-done = bf16[128,4096]{1,0:T(8,128)(2,1)} async-done(((bf16[128,1024]{1,0:T(8,128)(2,1)}), bf16[128,4096]{1,0:T(8,128)(2,1)}) %all-gather.20.cloned.1.call-update) | async-done | bytes 1048592 | tf_op jit(solution)/shard_map/all_gather | solution.py:33
  464.6 16.7 %fusion.30 = f32[128,4096]{1,0:T(8,128)} fusion(bf16[128,4096]{1,0:T(8,128)(2,1)} %all-gather.20.cloned.1.call-done, bf16[4096,4096]{1,0:T(8,128)(2,1)} %bitcast.85), kind=kOutput, calls=%fused_computation.56 | convolution fusion | flops 4294967296 | bytes 36700160 | tf_op jit(solution)/shard_map/dot_general | solution.py:32
  481.4 31.0 %reduce-scatter.20.cloned.1.call-done = f32[128,1024]{1,0:T(8,128)} async-done(((f32[128,4096]{1,0:T(8,128)}), f32[128,1024]{1,0:T(8,128)}) %reduce-scatter.20.cloned.1.call-update) | async-done | bytes 524304 | tf_op jit(solution)/shard_map/reduce_scatter | solution.py:35
  512.4 2.0 fusion.13
  514.4 28.1 %all-gather.22.cloned.1.call-done = bf16[128,4096]{1,0:T(8,128)(2,1)} async-done(((bf16[128,1024]{1,0:T(8,128)(2,1)}), bf16[128,4096]{1,0:T(8,128)(2,1)}) %all-gather.22.cloned.1.call-update) | async-done | bytes 1048592 | tf_op jit(solution)/shard_map/all_gather | solution.py:33
  542.5 16.7 %fusion.31 = f32[128,4096]{1,0:T(8,128)} fusion(bf16[128,4096]{1,0:T(8,128)(2,1)} %all-gather.22.cloned.1.call-done, bf16[4096,4096]{1,0:T(8,128)(2,1)} %bitcast.86), kind=kOutput, calls=%fused_computation.57 | convolution fusion | flops 4294967296 | bytes 36700160 | tf_op jit(solution)/shard_map/dot_general | solution.py:32
  559.3 31.0 %reduce-scatter.22.cloned.1.call-done = f32[128,1024]{1,0:T(8,128)} async-done(((f32[128,4096]{1,0:T(8,128)}), f32[128,1024]{1,0:T(8,128)}) %reduce-scatter.22.cloned.1.call-update) | async-done | bytes 524304 | tf_op jit(solution)/shard_map/reduce_scatter | solution.py:35
  590.3 2.1 fusion.19
  592.5 0.3 reduce-scatter.24.cloned.1.call-start
  592.8 27.8 %all-gather.24.cloned.1.call-done = bf16[128,4096]{1,0:T(8,128)(2,1)} async-done(((bf16[128,1024]{1,0:T(8,128)(2,1)}), bf16[128,4096]{1,0:T(8,128)(2,1)}) %all-gather.24.cloned.1.call-update) | async-done | bytes 1048592 | tf_op jit(solution)/shard_map/all_gather | solution.py:33
  620.6 16.7 %fusion.32 = f32[128,4096]{1,0:T(8,128)} fusion(bf16[128,4096]{1,0:T(8,128)(2,1)} %all-gather.24.cloned.1.call-done, bf16[4096,4096]{1,0:T(8,128)(2,1)} %bitcast.87), kind=kOutput, calls=%fused_computation.58 | convolution fusion | flops 4294967296 | bytes 36700160 | tf_op jit(solution)/shard_map/dot_general | solution.py:32
  637.4 31.0 %reduce-scatter.24.cloned.1.call-done = f32[128,1024]{1,0:T(8,128)} async-done(((f32[128,4096]{1,0:T(8,128)}), f32[128,1024]{1,0:T(8,128)}) %reduce-scatter.24.cloned.1.call-update) | async-done | bytes 524304 | tf_op jit(solution)/shard_map/reduce_scatter | solution.py:35
  668.4 2.1 fusion.9
  670.5 28.0 %all-gather.26.cloned.1.call-done = bf16[128,4096]{1,0:T(8,128)(2,1)} async-done(((bf16[128,1024]{1,0:T(8,128)(2,1)}), bf16[128,4096]{1,0:T(8,128)(2,1)}) %all-gather.26.cloned.1.call-update) | async-done | bytes 1048592 | tf_op jit(solution)/shard_map/all_gather | solution.py:33
  698.6 16.7 %fusion.33 = f32[128,4096]{1,0:T(8,128)} fusion(bf16[128,4096]{1,0:T(8,128)(2,1)} %all-gather.26.cloned.1.call-done, bf16[4096,4096]{1,0:T(8,128)(2,1)} %bitcast.88), kind=kOutput, calls=%fused_computation.59 | convolution fusion | flops 4294967296 | bytes 36700160 | tf_op jit(solution)/shard_map/dot_general | solution.py:32
  715.3 31.1 %reduce-scatter.26.cloned.1.call-done = f32[128,1024]{1,0:T(8,128)} async-done(((f32[128,4096]{1,0:T(8,128)}), f32[128,1024]{1,0:T(8,128)}) %reduce-scatter.26.cloned.1.call-update) | async-done | bytes 524304 | tf_op jit(solution)/shard_map/reduce_scatter | solution.py:35
  746.4 2.4 subtract_bitcast_fusion
  (39 shorter events, 0.6 us)
Async XLA Ops:
  7.2 3.8 copy-start
  7.2 50.0 %all-gather.10.cloned.1.call-start = ((), (), s32[]{:S(2)}) async-start(), calls=%async_computation.9 | async-start | bytes 1310720 | tf_op jit(solution)/shard_map/all_gather | solution.py:33
  7.2 15.2 %collective-permute-start = (f32[128,1024]{1,0:T(8,128)}, f32[128,1024]{1,0:T(8,128)S(1)}, u32[]{:S(2)}, u32[]{:S(2)}) collective-permute-start(f32[128,1024]{1,0:T(8,128)} %bitcast.90), channel_id=1, source_target_pairs={{0,16},{16,0},{1,17},{17,1},{2,18},{18,2},{3,19},{19,3},{4,20},{20... | collective-permute-start | bytes 1572872 | tf_op jit(solution)/shard_map/ppermute | solution.py:12
  27.6 77.4 %reduce-scatter.10.cloned.1.call-start = ((), (), s32[]{:S(2)}) async-start(), calls=%async_computation.10 | async-start | bytes 2621440 | tf_op jit(solution)/shard_map/reduce_scatter | solution.py:35
  50.4 23.6 %copy-start.6 = (s32[1,2]{1,0:T(1,128)S(1)}, s32[1,2]{1,0:T(1,128)}, u32[]{:S(2)}) copy-start(s32[1,2]{1,0:T(1,128)} %param.15) | copy-start | bytes 28
  50.4 54.6 %copy-start.2 = (f32[1,128,1024]{2,1,0:T(8,128)S(1)}, f32[1,128,1024]{2,1,0:T(8,128)}, u32[]{:S(2)}) copy-start(f32[1,128,1024]{2,1,0:T(8,128)} %param.11) | copy-start | bytes 1572868
  73.9 61.3 %all-gather.12.cloned.1.call-start = ((), (), s32[]{:S(2)}) async-start(), calls=%async_computation.11 | async-start | bytes 1310720 | tf_op jit(solution)/shard_map/all_gather | solution.py:33
  105.0 78.0 %copy-start.4 = (f32[128,1024]{1,0:T(8,128)S(1)}, f32[128,1024]{1,0:T(8,128)}, u32[]{:S(2)}) copy-start(f32[128,1024]{1,0:T(8,128)} %reduce-scatter.10.cloned.1.call-done) | copy-start | bytes 1572868
  106.9 76.0 %reduce-scatter.12.cloned.1.call-start = ((), (), s32[]{:S(2)}) async-start(), calls=%async_computation.12 | async-start | bytes 2621440 | tf_op jit(solution)/shard_map/reduce_scatter | solution.py:35
  151.9 61.1 %all-gather.14.cloned.1.call-start = ((), (), s32[]{:S(2)}) async-start(), calls=%async_computation.13 | async-start | bytes 1310720 | tf_op jit(solution)/shard_map/all_gather | solution.py:33
  184.9 75.9 %reduce-scatter.14.cloned.1.call-start = ((), (), s32[]{:S(2)}) async-start(), calls=%async_computation.14 | async-start | bytes 2621440 | tf_op jit(solution)/shard_map/reduce_scatter | solution.py:35
  229.8 109.2 %copy-start.3 = (f32[1,128,1024]{2,1,0:T(8,128)S(1)}, f32[1,128,1024]{2,1,0:T(8,128)}, u32[]{:S(2)}) copy-start(f32[1,128,1024]{2,1,0:T(8,128)} %param.10) | copy-start | bytes 1572868
  229.8 61.3 %all-gather.16.cloned.1.call-start = ((), (), s32[]{:S(2)}) async-start(), calls=%async_computation.15 | async-start | bytes 1310720 | tf_op jit(solution)/shard_map/all_gather | solution.py:33
  263.0 75.9 %reduce-scatter.16.cloned.1.call-start = ((), (), s32[]{:S(2)}) async-start(), calls=%async_computation.16 | async-start | bytes 2621440 | tf_op jit(solution)/shard_map/reduce_scatter | solution.py:35
  307.8 78.7 %all-gather.18.cloned.1.call-start = ((), (), s32[]{:S(2)}) async-start(), calls=%async_computation.17 | async-start | bytes 1310720 | tf_op jit(solution)/shard_map/all_gather | solution.py:33
  340.6 13.7 %collective-permute-start.1 = (f32[128,1024]{1,0:T(8,128)S(1)}, f32[128,1024]{1,0:T(8,128)S(1)}, u32[]{:S(2)}, u32[]{:S(2)}) collective-permute-start(f32[128,1024]{1,0:T(8,128)S(1)} %add_add_fusion), channel_id=1, source_target_pairs={{0,16},{16,0},{1,17},{17,1},{2,18},{18,2},{3,19},{19,3},{4,20},{20... | collective-permute-start | bytes 1572872 | tf_op jit(solution)/shard_map/ppermute | solution.py:12
  358.5 75.9 %reduce-scatter.18.cloned.1.call-start = ((), (), s32[]{:S(2)}) async-start(), calls=%async_computation.18 | async-start | bytes 2621440 | tf_op jit(solution)/shard_map/reduce_scatter | solution.py:35
  403.3 61.3 %all-gather.20.cloned.1.call-start = ((), (), s32[]{:S(2)}) async-start(), calls=%async_computation.19 | async-start | bytes 1310720 | tf_op jit(solution)/shard_map/all_gather | solution.py:33
  434.4 78.0 %copy-start.5 = (f32[128,1024]{1,0:T(8,128)S(1)}, f32[128,1024]{1,0:T(8,128)}, u32[]{:S(2)}) copy-start(f32[128,1024]{1,0:T(8,128)} %reduce-scatter.18.cloned.1.call-done) | copy-start | bytes 1572868
  436.3 76.1 %reduce-scatter.20.cloned.1.call-start = ((), (), s32[]{:S(2)}) async-start(), calls=%async_computation.20 | async-start | bytes 2621440 | tf_op jit(solution)/shard_map/reduce_scatter | solution.py:35
  481.3 61.2 %all-gather.22.cloned.1.call-start = ((), (), s32[]{:S(2)}) async-start(), calls=%async_computation.21 | async-start | bytes 1310720 | tf_op jit(solution)/shard_map/all_gather | solution.py:33
  514.4 75.9 %reduce-scatter.22.cloned.1.call-start = ((), (), s32[]{:S(2)}) async-start(), calls=%async_computation.22 | async-start | bytes 2621440 | tf_op jit(solution)/shard_map/reduce_scatter | solution.py:35
  559.3 61.3 %all-gather.24.cloned.1.call-start = ((), (), s32[]{:S(2)}) async-start(), calls=%async_computation.23 | async-start | bytes 1310720 | tf_op jit(solution)/shard_map/all_gather | solution.py:33
  592.5 75.9 %reduce-scatter.24.cloned.1.call-start = ((), (), s32[]{:S(2)}) async-start(), calls=%async_computation.24 | async-start | bytes 2621440 | tf_op jit(solution)/shard_map/reduce_scatter | solution.py:35
  620.6 128.3 %copy-start.1 = (s32[1024]{0:T(1024)S(1)}, s32[1024]{0:T(1024)}, u32[]{:S(2)}) copy-start(s32[1024]{0:T(1024)} %param.14) | copy-start | bytes 12292
  637.3 61.2 %all-gather.26.cloned.1.call-start = ((), (), s32[]{:S(2)}) async-start(), calls=%async_computation.25 | async-start | bytes 1310720 | tf_op jit(solution)/shard_map/all_gather | solution.py:33
  670.5 75.9 %reduce-scatter.26.cloned.1.call-start = ((), (), s32[]{:S(2)}) async-start(), calls=%async_computation.26 | async-start | bytes 2621440 | tf_op jit(solution)/shard_map/reduce_scatter | solution.py:35
Sparse Core Ops, SparseCore 0:
  27.7 29.3 all-gather.9
  74.0 30.9 reduce-scatter.9
  107.2 27.9 all-gather.11
  152.0 30.8 reduce-scatter.11
  185.1 27.9 all-gather.13
  229.9 30.9 reduce-scatter.13
  263.1 27.9 all-gather.15
  307.9 30.9 reduce-scatter.15
  358.6 27.9 all-gather.17
  403.4 30.9 reduce-scatter.17
  436.6 27.9 all-gather.19
  481.4 30.9 reduce-scatter.19
  514.5 27.9 all-gather.21
  559.4 30.9 reduce-scatter.21
  592.6 27.9 all-gather.23
  637.4 30.8 reduce-scatter.23
  670.6 27.9 all-gather.25
  715.4 30.9 reduce-scatter.25
where the time goes:
time: 762 us; the launch traced here: 756 us
  waiting for transfers between devices  526 us (69%)
  matrix products  150 us (20%)
  local copies, waits for them, and re-layouts  34.3 us (5%)
  other arithmetic  22.5 us (3%)
  between operations  16.5 us (2%)
    reduce_scatter x9, waiting for transfers between devices, apply_tile(): return lax.psum_scatter(partial_sum, 'row', scatter_dimension=1, tiled=True)  277 us
    all_gather x9, waiting for transfers between devices, apply_tile(): lax.all_gather(rounded, 'col', axis=1, tiled=True)  230 us
    dot_general x9, matrix products, apply_tile(): jnp.dot(lax.all_gather(rounded, 'col', axis=1, tiled=True), tile, preferr...  150 us
    unnamed x15, local copies, waits for them, and re-layouts  22.8 us
    ppermute x2, waiting for transfers between devices, swapped(): return lax.ppermute(value, axis, pairs)  18.4 us
    convert_element_type x9, other arithmetic, apply_tile(): rounded = field.astype(jnp.bfloat16)  16.9 us
  transfers between devices with their start and end apart: 20, of which 20 were waited for; matrix products, arithmetic and copies ran while one was open for 4% of the time, Pallas kernels for 0%

commit v1 on v0

v1 whole, which is shorter than its diff:
```python
import functools

import jax
import jax.numpy as jnp
from jax import lax
from jax.experimental import pallas as pl
from jax.experimental.pallas import tpu as pltpu
from jax.sharding import PartitionSpec as P

K = 4
GROUPS = 2
MESH = pl.DeviceIdType.MESH


def kernel(
    n_row, n_col, coef_ref, lam_ref, load_ref, tile_hbm, partner_ref, active_ref, x_ref, r_ref,
    tile, gathered, partial, core_in, far_out, far_in, peer0, peer1, select, flags, direction,
    tile_sem, own_send, pass_send, col_recv, core_send, core_recv, far_send, far_recv, peer_send, peer_recv,
):
    rows, width = lam_ref.shape
    part = rows // GROUPS
    n_far = n_row // 2
    applies = 2 * K + 1
    hub = n_col == 4
    body = lax.axis_index("body")
    row = lax.axis_index("row")
    col = lax.axis_index("col")
    core = row % 2
    far = row // 2
    core_peer = row + 1 - 2 * core
    if hub:
        col_mate = col + 1 - 2 * (col % 2)
        inner_over = 2 - col // 2
        end_over = 3 - 3 * (col // 2)
        order = [col, col_mate, inner_over, end_over]
        targets = [col_mate, inner_over]
    else:
        order = [(col + shift) % n_col for shift in range(n_col)]
        targets = [(col + shift) % n_col for shift in range(1, n_col)]
    inner = ((col + 1) // 2) % 2 == 1

    tile_copy = pltpu.make_async_copy(tile_hbm, tile, tile_sem)
    tile_copy.start()

    barrier = pltpu.get_barrier_semaphore()
    for shift in range(1, n_col):
        pl.semaphore_signal(barrier, inc=1, device_id={"col": (col + shift) % n_col}, device_id_type=MESH)
    for shift in range(1, n_row):
        pl.semaphore_signal(barrier, inc=1, device_id={"row": (row + shift) % n_row}, device_id_type=MESH)
    pl.semaphore_signal(barrier, inc=1, device_id={"body": 1 - body}, device_id_type=MESH)
    pl.semaphore_wait(barrier, n_col + n_row - 1)

    def peer_copy(source, target, slot):
        return pltpu.make_async_remote_copy(
            src_ref=source, dst_ref=target, send_sem=peer_send.at[slot], recv_sem=peer_recv.at[slot],
            device_id={"body": 1 - body}, device_id_type=MESH,
        )

    def col_copy(parity, group, source, target, send_sem):
        block = gathered.at[parity, group, source]
        return pltpu.make_async_remote_copy(
            src_ref=block, dst_ref=block, send_sem=send_sem, recv_sem=col_recv.at[parity, group, source],
            device_id={"col": target}, device_id_type=MESH,
        )

    def own_copies(parity, group):
        return [
            col_copy(parity, group, col, target, own_send.at[group, at]) for at, target in enumerate(targets)
        ]

    def core_copy(parity, group):
        return pltpu.make_async_remote_copy(
            src_ref=partial.at[group, 1 - core], dst_ref=core_in.at[parity, group],
            send_sem=core_send.at[group], recv_sem=core_recv.at[parity, group],
            device_id={"row": core_peer}, device_id_type=MESH,
        )

    def far_copy(parity, group, shift):
        return pltpu.make_async_remote_copy(
            src_ref=far_out.at[group, shift - 1], dst_ref=far_in.at[parity, group, shift - 1],
            send_sem=far_send.at[group, shift - 1], recv_sem=far_recv.at[parity, group, shift - 1],
            device_id={"row": ((far + shift) % n_far) * 2 + core}, device_id_type=MESH,
        )

    first = peer_copy(lam_ref, peer0, 0)
    first.start()

    which = jnp.broadcast_to(partner_ref[...] % width, (width, width))
    select[...] = jnp.where(
        lax.broadcasted_iota(jnp.int32, (width, width), 0) == which, 1.0, 0.0
    ).astype(jnp.bfloat16)
    active = active_ref[...].astype(jnp.float32)
    spread = jnp.broadcast_to(active, (16, width)).astype(jnp.bfloat16)
    moved = jnp.dot(spread, select[...], preferred_element_type=jnp.float32)[:1]
    flags[...] = jnp.where(body == 0, active, moved)
    sign = (1 - 2 * body).astype(jnp.float32)
    r_ref[...] = load_ref[...]
    direction[...] = jnp.zeros_like(direction)

    def clamp(lam, peer):
        high = peer.astype(jnp.bfloat16)
        rest = peer - high.astype(jnp.float32)
        middle_piece = rest.astype(jnp.bfloat16)
        low = (rest - middle_piece.astype(jnp.float32)).astype(jnp.bfloat16)
        mate = jnp.dot(high, select[...], preferred_element_type=jnp.float32)
        mate = mate + jnp.dot(middle_piece, select[...], preferred_element_type=jnp.float32)
        mate = mate + jnp.dot(low, select[...], preferred_element_type=jnp.float32)
        middle = 0.5 * (lam + mate)
        normal = 0.5 * sign * (lam - mate)
        normal = jnp.where(flags[...] > 0.5, jnp.maximum(normal, 0.0), normal)
        return middle + sign * normal

    def multiply(parity, group, source, start):
        def one(q, carry):
            columns = pl.ds(pl.multiple_of(q * width, width), width)
            depth = pl.ds(pl.multiple_of(source * width, width), width)
            product = jnp.dot(gathered[parity, group, source], tile[depth, columns], preferred_element_type=jnp.float32)
            if start:
                partial[group, q % 2, q // 2] = product
            else:
                partial[group, q % 2, q // 2] += product
            return carry

        lax.fori_loop(0, n_row, one, 0)

    def begin(parity, group, value):
        gathered[parity, group, col] = value.astype(jnp.bfloat16)
        for copy in own_copies(parity, group):
            copy.start()

    first.wait()
    for group in range(GROUPS):
        band = pl.ds(group * part, part)
        start = clamp(lam_ref[band, :], peer0[band, :])
        x_ref[band, :] = start
        begin(0, group, start)
    tile_copy.wait()

    def half_step(h, carry):
        group = h % GROUPS
        time = h // GROUPS
        parity = time % 2
        late = (h + GROUPS - 1) % GROUPS
        late_time = (h + GROUPS - 1) // GROUPS - 1
        late_parity = (late_time + 2) % 2
        live = h < applies * GROUPS

        @pl.when(live)
        def _():
            multiply(parity, group, order[0], True)

        @pl.when(h >= 1)
        def _():
            core_copy(late_parity, late).wait()
            for shift in range(1, n_far):
                other = (far + shift) % n_far
                far_out[late, shift - 1] = partial[late, core, other] + core_in[late_parity, late, other]
                far_copy(late_parity, late, shift).start()

        def take(at):
            source = order[at]
            col_copy(parity, group, source, source, own_send.at[group, 0]).wait_recv()
            if hub and at >= 2:
                @pl.when(inner)
                def _():
                    col_copy(parity, group, source, col_mate, pass_send.at[group, at - 2]).start()
            multiply(parity, group, source, False)

        @pl.when(live)
        def _():
            for at in range(1, n_col - 1):
                take(at)

        @pl.when(h >= 1)
        def _():
            total = partial[late, core, far] + core_in[late_parity, late, far]
            for shift in range(1, n_far):
                far_copy(late_parity, late, shift).wait()
                total = total + far_in[late_parity, late, shift - 1]
            for copy in own_copies(late_parity, late):
                copy.wait_send()
            if hub:
                @pl.when(inner)
                def _():
                    for at in range(2):
                        col_copy(late_parity, late, order[at + 2], col_mate, pass_send.at[late, at]).wait_send()
            band = pl.ds(pl.multiple_of(late * part, part), part)
            resid = r_ref[band, :] - total
            r_ref[band, :] = resid

            @pl.when(late_time != 2 * K)
            def _():
                step = late_time % K
                move = coef_ref[step] * direction[band, :] + coef_ref[K + step] * resid
                direction[band, :] = move
                answer = x_ref[band, :] + move
                x_ref[band, :] = answer

                @pl.when(late_time != K - 1)
                def _():
                    begin(1 - late_parity, late, move)

                @pl.when(late_time == K - 1)
                def _():
                    exchange = peer_copy(x_ref.at[band, :], peer1.at[band, :], 1 + late)
                    exchange.start()
                    exchange.wait()
                    again = clamp(x_ref[band, :], peer1[band, :])
                    x_ref[band, :] = again
                    r_ref[band, :] = load_ref[band, :]
                    begin(1 - late_parity, late, again)

        @pl.when(live)
        def _():
            take(n_col - 1)
            core_copy(parity, group).start()

        return carry

    lax.fori_loop(0, applies * GROUPS + 1, half_step, 0)


def coefficients(bounds):
    lower = bounds[0, 0].astype(jnp.float32)
    upper = bounds[0, 1].astype(jnp.float32)
    theta = 0.5 * (upper + lower)
    delta = 0.5 * (upper - lower)
    sigma = theta / delta
    rho = delta / theta
    keep, add = [jnp.zeros_like(theta)], [1.0 / theta]
    for _ in range(K - 1):
        rho_new = 1.0 / (2.0 * sigma - rho)
        keep.append(rho_new * rho)
        add.append(2.0 * rho_new / delta)
        rho = rho_new
    return jnp.stack(keep + add)


def per_device(n_row, n_col, lam_start, load, operator, partner, active, bounds):
    rows, width = lam_start.shape[1:]
    tile = operator.reshape(operator.shape[1], operator.shape[2] * operator.shape[4])
    part = rows // GROUPS
    n_far = n_row // 2
    f32, bf16 = jnp.float32, jnp.bfloat16
    vmem = pl.BlockSpec(memory_space=pltpu.VMEM)
    dma = pltpu.SemaphoreType.DMA
    flops = 2 * (2 * K + 1) * rows * tile.shape[0] * tile.shape[1]
    answer, resid = pl.pallas_call(
        functools.partial(kernel, n_row, n_col),
        out_shape=[jax.ShapeDtypeStruct((rows, width), f32)] * 2,
        in_specs=[
            pl.BlockSpec(memory_space=pltpu.SMEM), vmem, vmem, pl.BlockSpec(memory_space=pl.ANY), vmem, vmem,
        ],
        out_specs=[vmem, vmem],
        scratch_shapes=[
            pltpu.VMEM(tile.shape, bf16),
            pltpu.VMEM((2, GROUPS, n_col, part, width), bf16),
            pltpu.VMEM((GROUPS, 2, n_far, part, width), f32),
            pltpu.VMEM((2, GROUPS, n_far, part, width), f32),
            pltpu.VMEM((GROUPS, n_far - 1, part, width), f32),
            pltpu.VMEM((2, GROUPS, n_far - 1, part, width), f32),
            pltpu.VMEM((rows, width), f32),
            pltpu.VMEM((rows, width), f32),
            pltpu.VMEM((width, width), bf16),
            pltpu.VMEM((1, width), f32),
            pltpu.VMEM((rows, width), f32),
            dma,
            dma((GROUPS, n_col - 1)),
            dma((GROUPS, 2)),
            dma((2, GROUPS, n_col)),
            dma((GROUPS,)),
            dma((2, GROUPS)),
            dma((GROUPS, n_far - 1)),
            dma((2, GROUPS, n_far - 1)),
            dma((1 + GROUPS,)),
            dma((1 + GROUPS,)),
        ],
        compiler_params=pltpu.CompilerParams(
            collective_id=0, has_side_effects=True, vmem_limit_bytes=58 * 1024 * 1024
        ),
        cost_estimate=pl.CostEstimate(flops=flops, bytes_accessed=2 * tile.size, transcendentals=0),
    )(coefficients(bounds), lam_start[0], load[0], tile, partner, active[None])
    return (answer[None], resid[None])


def solution(mesh):
    return jax.shard_map(
        functools.partial(per_device, mesh.shape["row"], mesh.shape["col"]),
        mesh=mesh,
        in_specs=(
            P("body", None, ("row", "col")),
            P("body", None, ("row", "col")),
            P("body", "row", None, "col", None),
            P("body", ("row", "col")),
            P(("row", "col")),
            P("body", None),
        ),
        out_specs=(P("body", None, ("row", "col")), P("body", None, ("row", "col"))),
        check_vma=False,
    )
```

time: 762 us -> 322 us (0.42)
  waiting for transfers between devices: 526 us -> 0 us
  Pallas kernels: 0 us -> 291 us
  matrix products: 150 us -> 0 us
  other arithmetic: 22.5 us -> 0 us
  between operations: 16.5 us -> 2.31 us
    pallas_call x0 -> x1, Pallas kernels: none -> 291 us  [per_device(): pl.pallas_call(functools.partial(kernel, n_row, n_col), out_shape=[jax.Sh...]
    reduce_scatter x9 -> x0, waiting for transfers between devices: 277 us -> none  [apply_tile(): return lax.psum_scatter(partial_sum, 'row', scatter_dimension=1, tiled=True)]
    all_gather x9 -> x0, waiting for transfers between devices: 230 us -> none  [apply_tile(): lax.all_gather(rounded, 'col', axis=1, tiled=True)]
    dot_general x9 -> x0, matrix products: 150 us -> none  [apply_tile(): jnp.dot(lax.all_gather(rounded, 'col', axis=1, tiled=True), tile, preferr...]
    ppermute x2 -> x0, waiting for transfers between devices: 18.4 us -> none  [swapped(): return lax.ppermute(value, axis, pairs)]
    convert_element_type x9 -> x0, other arithmetic: 16.9 us -> none  [apply_tile(): rounded = field.astype(jnp.bfloat16)]
    gather x5 -> x0, local copies, waits for them, and re-layouts: 10.5 us -> none  [the longest x4 6.02 us: clamp_local(): mate = jnp.take(peer, local, axis=1)]
    unnamed x15 -> x3, local copies, waits for them, and re-layouts: 22.8 us -> 26.5 us
  transfers between devices with their start and end apart: 20 -> 0, of which waited for: 20 -> 0; matrix products, arithmetic and copies ran while one was open for 4% -> 0% of each run, Pallas kernels for 0% -> 0%
where the time goes in v1:
time: 322 us
  Pallas kernels  291 us (90%)
  local copies, waits for them, and re-layouts  28.4 us (9%)
    pallas_call x1, Pallas kernels, per_device(): pl.pallas_call(functools.partial(kernel, n_row, n_col), out_shape=[jax.Sh...  291 us
    unnamed x3, local copies, waits for them, and re-layouts  26.5 us

profile of v1, /device:TPU:0, one launch (start us, length us, event | category | flops | bytes accessed | tf_op | source)
XLA Modules:
  0.0 321.9 jit_solution(11006833759754436509)
XLA Ops:
  0.6 1.3 fusion
  3.6 0.6 stack.31.coef_ref
  4.2 22.7 %copy.8 = bf16[512,8,4,1024]{3,1,2,0:T(8,128)(2,1)} copy(bf16[512,8,4,1024]{3,2,1,0:T(4,128)(2,1)} %bitcast.18) | data formatting | bytes 67108864
  27.0 291.2 %shard_map.77 = (f32[128,1024]{1,0:T(8,128)}, f32[128,1024]{1,0:T(8,128)}) custom-call(f32[8]{0:T(128)} %stack.31.coef_ref, f32[128,1024]{1,0:T(8,128)} %bitcast.22, f32[128,1024]{1,0:T(8,128)} %bitcast.23, bf16[4096,4096]{1,0:T(8,128)(2,1)} %bitcast.19, s32[1,1024]{1,0:T(1,128)} %partner_ref.1, s32[1,1024]{1,0:T(1,128)} %bitcast.24), custom_call_target="tpu_custom_call" | custom-call | flops 38654705664 | bytes 33554432 | tf_op jit(solution)/shard_map/pallas_call | solution.py:248
  318.1 1.9 copy.11
  320.0 1.9 copy.12

commit v2 on v1

--- a/solution.py
+++ b/solution.py
@@ -82,8 +82,10 @@
             device_id={"row": ((far + shift) % n_far) * 2 + core}, device_id_type=MESH,
         )
 
-    first = peer_copy(lam_ref, peer0, 0)
-    first.start()
+    bands = [pl.ds(group * part, part) for group in range(GROUPS)]
+    first = [peer_copy(lam_ref.at[band, :], peer0.at[band, :], GROUPS + at) for at, band in enumerate(bands)]
+    for copy in first:
+        copy.start()
 
     which = jnp.broadcast_to(partner_ref[...] % width, (width, width))
     select[...] = jnp.where(
@@ -110,27 +112,28 @@
         normal = jnp.where(flags[...] > 0.5, jnp.maximum(normal, 0.0), normal)
         return middle + sign * normal
 
-    def multiply(parity, group, source, start):
-        def one(q, carry):
-            columns = pl.ds(pl.multiple_of(q * width, width), width)
+    def multiply(parity, group, source, start, low=0, high=n_row):
+        def one(at, carry):
+            to_core = (core + 1 + at // n_far) % 2
+            to_far = (far + 1 + at) % n_far
+            columns = pl.ds(pl.multiple_of((to_far * 2 + to_core) * width, width), width)
             depth = pl.ds(pl.multiple_of(source * width, width), width)
             product = jnp.dot(gathered[parity, group, source], tile[depth, columns], preferred_element_type=jnp.float32)
             if start:
-                partial[group, q % 2, q // 2] = product
+                partial[group, to_core, to_far] = product
             else:
-                partial[group, q % 2, q // 2] += product
+                partial[group, to_core, to_far] += product
             return carry
 
-        lax.fori_loop(0, n_row, one, 0)
+        lax.fori_loop(low, high, one, 0)
 
     def begin(parity, group, value):
         gathered[parity, group, col] = value.astype(jnp.bfloat16)
         for copy in own_copies(parity, group):
             copy.start()
 
-    first.wait()
-    for group in range(GROUPS):
-        band = pl.ds(group * part, part)
+    for group, band in enumerate(bands):
+        first[group].wait()
         start = clamp(lam_ref[band, :], peer0[band, :])
         x_ref[band, :] = start
         begin(0, group, start)
@@ -145,10 +148,6 @@
         late_parity = (late_time + 2) % 2
         live = h < applies * GROUPS
 
-        @pl.when(live)
-        def _():
-            multiply(parity, group, order[0], True)
-
         @pl.when(h >= 1)
         def _():
             core_copy(late_parity, late).wait()
@@ -157,19 +156,42 @@
                 far_out[late, shift - 1] = partial[late, core, other] + core_in[late_parity, late, other]
                 far_copy(late_parity, late, shift).start()
 
+        @pl.when(live & (time == K))
+        def _():
+            band = pl.ds(pl.multiple_of(group * part, part), part)
+            peer_copy(x_ref.at[band, :], peer1.at[band, :], group).wait()
+            again = clamp(x_ref[band, :], peer1[band, :])
+            x_ref[band, :] = again
+            r_ref[band, :] = load_ref[band, :]
+            begin(parity, group, again)
+
+        def arrive(at):
+            col_copy(parity, group, order[at], order[at], own_send.at[group, 0]).wait_recv()
+
+        def pass_on(at):
+            @pl.when(inner)
+            def _():
+                arrive(at)
+                col_copy(parity, group, order[at], col_mate, pass_send.at[group, at - 2]).start()
+
         def take(at):
-            source = order[at]
-            col_copy(parity, group, source, source, own_send.at[group, 0]).wait_recv()
             if hub and at >= 2:
-                @pl.when(inner)
+                @pl.when(jnp.logical_not(inner))
                 def _():
-                    col_copy(parity, group, source, col_mate, pass_send.at[group, at - 2]).start()
-            multiply(parity, group, source, False)
+                    arrive(at)
+            else:
+                arrive(at)
 
         @pl.when(live)
         def _():
+            if hub:
+                pass_on(2)
+            multiply(parity, group, order[0], True)
+            if hub:
+                pass_on(3)
             for at in range(1, n_col - 1):
                 take(at)
+                multiply(parity, group, order[at], False)
 
         @pl.when(h >= 1)
         def _():
@@ -202,18 +224,14 @@
 
                 @pl.when(late_time == K - 1)
                 def _():
-                    exchange = peer_copy(x_ref.at[band, :], peer1.at[band, :], 1 + late)
-                    exchange.start()
-                    exchange.wait()
-                    again = clamp(x_ref[band, :], peer1[band, :])
-                    x_ref[band, :] = again
-                    r_ref[band, :] = load_ref[band, :]
-                    begin(1 - late_parity, late, again)
+                    peer_copy(x_ref.at[band, :], peer1.at[band, :], late).start()
 
         @pl.when(live)
         def _():
             take(n_col - 1)
+            multiply(parity, group, order[n_col - 1], False, 0, n_far)
             core_copy(parity, group).start()
+            multiply(parity, group, order[n_col - 1], False, n_far, n_row)
 
         return carry
 
@@ -272,8 +290,8 @@
             dma((2, GROUPS)),
             dma((GROUPS, n_far - 1)),
             dma((2, GROUPS, n_far - 1)),
-            dma((1 + GROUPS,)),
-            dma((1 + GROUPS,)),
+            dma((2 * GROUPS,)),
+            dma((2 * GROUPS,)),
         ],
         compiler_params=pltpu.CompilerParams(
             collective_id=0, has_side_effects=True, vmem_limit_bytes=58 * 1024 * 1024

time: 322 us -> 285 us (0.89)
  Pallas kernels: 291 us -> 254 us
    pallas_call x1, Pallas kernels: 291 us -> 254 us  [per_device(): pl.pallas_call(functools.partial(kernel, n_row, n_col), out_shape=[jax.Sh...]
where the time goes in v2:
time: 285 us
  Pallas kernels  254 us (89%)
  local copies, waits for them, and re-layouts  28.4 us (10%)
    pallas_call x1, Pallas kernels, per_device(): pl.pallas_call(functools.partial(kernel, n_row, n_col), out_shape=[jax.Sh...  254 us
    unnamed x3, local copies, waits for them, and re-layouts  26.5 us

profile of v2, /device:TPU:0, one launch (start us, length us, event | category | flops | bytes accessed | tf_op | source)
XLA Modules:
  0.0 285.0 jit_solution(15299083022884758684)
XLA Ops:
  0.6 1.3 fusion
  3.6 0.6 stack.31.coef_ref
  4.2 22.7 %copy.8 = bf16[512,8,4,1024]{3,1,2,0:T(8,128)(2,1)} copy(bf16[512,8,4,1024]{3,2,1,0:T(4,128)(2,1)} %bitcast.18) | data formatting | bytes 67108864
  27.0 254.3 %shard_map.77 = (f32[128,1024]{1,0:T(8,128)}, f32[128,1024]{1,0:T(8,128)}) custom-call(f32[8]{0:T(128)} %stack.31.coef_ref, f32[128,1024]{1,0:T(8,128)} %bitcast.22, f32[128,1024]{1,0:T(8,128)} %bitcast.23, bf16[4096,4096]{1,0:T(8,128)(2,1)} %bitcast.19, s32[1,1024]{1,0:T(1,128)} %partner_ref.1, s32[1,1024]{1,0:T(1,128)} %bitcast.24), custom_call_target="tpu_custom_call" | custom-call | flops 38654705664 | bytes 33554432 | tf_op jit(solution)/shard_map/pallas_call | solution.py:266
  281.2 1.9 copy.11
  283.1 1.9 copy.12

commit v3 on v2

--- a/solution.py
+++ b/solution.py
@@ -14,7 +14,7 @@
 
 def kernel(
     n_row, n_col, coef_ref, lam_ref, load_ref, tile_hbm, partner_ref, active_ref, x_ref, r_ref,
-    tile, gathered, partial, core_in, far_out, far_in, peer0, peer1, select, flags, direction,
+    tile, raw, wide, gathered, partial, core_in, far_out, far_in, peer0, peer1, select, flags, direction,
     tile_sem, own_send, pass_send, col_recv, core_send, core_recv, far_send, far_recv, peer_send, peer_recv,
 ):
     rows, width = lam_ref.shape
@@ -39,8 +39,15 @@
         targets = [(col + shift) % n_col for shift in range(1, n_col)]
     inner = ((col + 1) // 2) % 2 == 1
 
-    tile_copy = pltpu.make_async_copy(tile_hbm, tile, tile_sem)
-    tile_copy.start()
+    chunk = raw.shape[1]
+    chunks = tile_hbm.shape[0] // chunk
+
+    def raw_copy(at):
+        return pltpu.make_async_copy(
+            tile_hbm.at[pl.ds(pl.multiple_of(at * chunk, chunk), chunk)], raw.at[at % 2], tile_sem.at[at % 2]
+        )
+
+    raw_copy(0).start()
 
     barrier = pltpu.get_barrier_semaphore()
     for shift in range(1, n_col):
@@ -132,12 +139,29 @@
         for copy in own_copies(parity, group):
             copy.start()
 
+    def sort_chunk(at, carry):
+        @pl.when(at + 1 < chunks)
+        def _():
+            raw_copy(at + 1).start()
+
+        raw_copy(at).wait()
+        depth = pl.ds(pl.multiple_of(at * chunk, chunk), chunk)
+        for lane in range(width // 128):
+            slot = lane % 2
+            wide[slot] = raw[at % 2, :, :, lane * 128:(lane + 1) * 128].astype(jnp.float32)
+            flat = wide.at[slot].reshape(chunk * n_row, 128)
+            for q in range(n_row):
+                tile[depth, q * width + lane * 128:q * width + (lane + 1) * 128] = flat[
+                    pl.ds(q, chunk, stride=n_row), :
+                ].astype(jnp.bfloat16)
+        return carry
+
+    lax.fori_loop(0, chunks, sort_chunk, 0)
     for group, band in enumerate(bands):
         first[group].wait()
         start = clamp(lam_ref[band, :], peer0[band, :])
         x_ref[band, :] = start
         begin(0, group, start)
-    tile_copy.wait()
 
     def half_step(h, carry):
         group = h % GROUPS
@@ -256,13 +280,14 @@
 
 def per_device(n_row, n_col, lam_start, load, operator, partner, active, bounds):
     rows, width = lam_start.shape[1:]
-    tile = operator.reshape(operator.shape[1], operator.shape[2] * operator.shape[4])
+    tile = operator.reshape(operator.shape[1], operator.shape[2], operator.shape[4])
+    chunk = min(256, tile.shape[0])
     part = rows // GROUPS
     n_far = n_row // 2
     f32, bf16 = jnp.float32, jnp.bfloat16
     vmem = pl.BlockSpec(memory_space=pltpu.VMEM)
     dma = pltpu.SemaphoreType.DMA
-    flops = 2 * (2 * K + 1) * rows * tile.shape[0] * tile.shape[1]
+    flops = 2 * (2 * K + 1) * rows * tile.size
     answer, resid = pl.pallas_call(
         functools.partial(kernel, n_row, n_col),
         out_shape=[jax.ShapeDtypeStruct((rows, width), f32)] * 2,
@@ -271,7 +296,9 @@
         ],
         out_specs=[vmem, vmem],
         scratch_shapes=[
-            pltpu.VMEM(tile.shape, bf16),
+            pltpu.VMEM((tile.shape[0], n_row * width), bf16),
+            pltpu.VMEM((2, chunk, n_row, width), bf16),
+            pltpu.VMEM((2, chunk, n_row, 128), f32),
             pltpu.VMEM((2, GROUPS, n_col, part, width), bf16),
             pltpu.VMEM((GROUPS, 2, n_far, part, width), f32),
             pltpu.VMEM((2, GROUPS, n_far, part, width), f32),
@@ -282,7 +309,7 @@
             pltpu.VMEM((width, width), bf16),
             pltpu.VMEM((1, width), f32),
             pltpu.VMEM((rows, width), f32),
-            dma,
+            dma((2,)),
             dma((GROUPS, n_col - 1)),
             dma((GROUPS, 2)),
             dma((2, GROUPS, n_col)),

time: 285 us -> 281 us (0.986)
  local copies, waits for them, and re-layouts: 28.4 us -> 5.71 us
  Pallas kernels: 254 us -> 273 us
    unnamed x3 -> x2, local copies, waits for them, and re-layouts: 26.5 us -> 3.77 us
    pallas_call x1, Pallas kernels: 254 us -> 273 us  [per_device(): pl.pallas_call(functools.partial(kernel, n_row, n_col), out_shape=[jax.Sh...]
where the time goes in v3:
time: 281 us
  Pallas kernels  273 us (97%)
  local copies, waits for them, and re-layouts  5.71 us (2%)
    pallas_call x1, Pallas kernels, per_device(): pl.pallas_call(functools.partial(kernel, n_row, n_col), out_shape=[jax.Sh...  273 us

profile of v3, /device:TPU:0, one launch (start us, length us, event | category | flops | bytes accessed | tf_op | source)
XLA Modules:
  0.0 280.7 jit_solution(3737397387987783916)
XLA Ops:
  0.6 1.3 fusion
  3.6 0.6 stack.31.coef_ref
  4.2 272.7 %shard_map.77 = (f32[128,1024]{1,0:T(8,128)}, f32[128,1024]{1,0:T(8,128)}) custom-call(f32[8]{0:T(128)} %stack.31.coef_ref, f32[128,1024]{1,0:T(8,128)} %bitcast.18, f32[128,1024]{1,0:T(8,128)} %bitcast.19, bf16[4096,4,1024]{2,1,0:T(4,128)(2,1)} %bitcast.17, s32[1,1024]{1,0:T(1,128)} %partner_ref.1, s32[1,1024]{1,0:T(1,128)} %bitcast.20), custom_call_target="tpu_custom_call" | custom-call | flops 38654705664 | bytes 33554432 | tf_op jit(solution)/shard_map/pallas_call | solution.py:291
  277.0 1.9 copy.10
  278.9 1.9 copy.11
